TPU v7x, 128 devices: a whole 4x4x4 slice. The times are simulated.
128 devices in a mesh: ctx: 16 (over y_lo, z, core), fsdp: 8 (over x, y_hi).
Axes of the slice: x: 4, y: 4 (y_hi: 2, y_lo: 2; y = y_hi * 2 + y_lo), z: 4, core: 2. Of those that a mesh axis runs over, the one named last changes fastest.
Arguments:
- tokens: bfloat16 [2, 8, 2048, 1024], P(None, 'fsdp', 'ctx')
- cotangent: bfloat16 [2, 8, 2048, 1024], P(None, 'fsdp', 'ctx')
- dest: int32 [2, 8, 2048], P(None, 'fsdp', 'ctx'), may hold values from 0 to 2047, as said below
- lengths: int32 [2, 8, 8], P(None, 'fsdp'), may hold values from 1 to 1024, as said below
- attn_weight: float32 [1024, 4096], P('fsdp')
- attn_first: float32 [1024, 4096], P('fsdp'), may hold values from -0.00048828125 to 0.00048828125
- attn_second: float32 [1024, 4096], P('fsdp'), may hold values from 7.9395324e-11 to 3.175813e-10
- ffn_weight: float32 [1024, 8192], P('fsdp')
- ffn_first: float32 [1024, 8192], P('fsdp'), may hold values from -0.00048828125 to 0.00048828125
- ffn_second: float32 [1024, 8192], P('fsdp'), may hold values from 7.9395324e-11 to 3.175813e-10
- vectors: float32 [12, 1024], P(None, 'fsdp')
- vec_first: float32 [12, 1024], P(None, 'fsdp'), may hold values from -0.0048828125 to 0.0048828125
- vec_second: float32 [12, 1024], P(None, 'fsdp'), may hold values from 2.3818598e-09 to 9.527439e-09
Outputs:
- layer_output: bfloat16 [2, 8, 2048, 1024], P(None, 'fsdp', 'ctx')
- input_grad: bfloat16 [2, 8, 2048, 1024], P(None, 'fsdp', 'ctx')
- grad_norm: float32 [], replicated
- attn_new: float32 [1024, 4096], P('fsdp')
- attn_first_new: float32 [1024, 4096], P('fsdp')
- attn_second_new: float32 [1024, 4096], P('fsdp')
- ffn_new: float32 [1024, 8192], P('fsdp')
- ffn_first_new: float32 [1024, 8192], P('fsdp')
- ffn_second_new: float32 [1024, 8192], P('fsdp')
- vec_new: float32 [12, 1024], P(None, 'fsdp')
- vec_first_new: float32 [12, 1024], P(None, 'fsdp')
- vec_second_new: float32 [12, 1024], P(None, 'fsdp')
- attn_copy: bfloat16 [1024, 4096], P('fsdp')
- ffn_copy: bfloat16 [1024, 8192], P('fsdp')
- output_bias_grad: float32 [1024], P('fsdp')
Inputs may be any that keep to these rules, and one draw needn't show every extreme that they name: Within each micro-batch and fsdp index, dest is a permutation of the pack's slots; slot s lies on ctx device s // 128, and each ctx device's given tokens go exactly 8 to each ctx device. The lengths of a pack sum to at most 2048; one of them is exactly 1024; sequences fill the packed slots in order and the rest is padding.
All inputs are finite; a program needn't handle non-finite values.
Results may differ from a plain program's by a relative error of at most 0.03.
Values may be sent and summed in bfloat16 or wider, within the bound.
A program may use at most 320 MiB of HBM per device.

v0:
```python
import math

import jax
import jax.numpy as jnp
from jax import lax
from jax.experimental import pallas as pl
from jax.experimental.pallas import tpu as pltpu
from jax.sharding import Mesh, PartitionSpec as P

HEADS = 16
HEAD = 64
STEP = 10
MB = 2
TOK = 128
ROWS = MB * TOK
D = 1024
FF = 4096
N_CTX = 16
N_FSDP = 8
PACK = 2048
SENT = 208

NORM_EPS = 1e-05
CLIP_NORM = 1.0
BETA_FIRST = 0.9
BETA_SECOND = 0.999
ADAM_EPS = 1e-08
WEIGHT_DECAY = 0.01
RATE_VECTOR = 0.3
ATTN_RATE_SCALE = 3.0
NEG_LARGE = -1e30
SCALE2 = HEAD ** (-0.5) * math.log2(math.e)
SCALE = HEAD ** (-0.5)
CONTRACT_ROWS = (((0,), (0,)), ((), ()))
CONTRACT_COLS = (((1,), (1,)), ((), ()))
CTX = ("yl", "z", "core")
FSDP = ("x", "yh")
ALL = ("x", "yh", "yl", "z", "core")
BLK = 256
NBLK = PACK // BLK
f32 = jnp.float32
bf16 = jnp.bfloat16


def dot(a, b):
    return jnp.dot(a, b, preferred_element_type=f32)


def dot_nt(a, b):
    return lax.dot_general(a, b, CONTRACT_COLS, preferred_element_type=f32)


def dot_tn(a, b):
    return lax.dot_general(a, b, CONTRACT_ROWS, preferred_element_type=f32)


MESH_ID = pl.DeviceIdType.MESH
COLS = 512
N_BLK = 4
ORDERS = (("x", "z", "y"), ("z", "y", "x"), ("y", "x", "z"))
EARLY = ((0, 0), (1, 0), (2, 0), (0, 1), (1, 1), (2, 1), (0, 2), (1, 2), (2, 2))
N_EARLY = (3, 3, 3)
EARLY_PRODUCT = ((2, 0), (2, 512), (2, 1024), (2, 1536), (3, 0), (3, 512), (3, 1024), (3, 1536), (1, 0))
PRODUCT = {part_block: product for part_block, product in zip(EARLY, EARLY_PRODUCT)}
PRODUCT.update({(p, N_EARLY[p]): (0, p * COLS) for p in range(3)})
PART_AT = (0, 2048, 4096, 6144)
VEC_AT = 3072
WIDTHS = (1536, 512, 2048, 2048)
OFFSETS = (0, 1536, 2048, 4096)
HALF_Z = 3072
TASKS = {}
for _n, _at in enumerate((2, 2, 2, 5, 5, 5, 8, 8, 8)):
    TASKS.setdefault(_at, []).append(("relay", *EARLY[_n]))
for _n, _at in enumerate((7, 7, 7, 10, 10, 10, 13, 13, 13)):
    TASKS.setdefault(_at, []).append((0, *EARLY[_n]))


def coordinate(axis):
    if axis == "y":
        return lax.axis_index("yh") * 2 + lax.axis_index("yl")
    return lax.axis_index(axis)


def peer(axis, step):
    at = lax.rem(coordinate(axis) + step, 4)
    if axis == "y":
        return {"yh": at // 2, "yl": lax.rem(at, 2)}, at
    return {axis: at}, at


def pick(ref, axis, at, dims):
    index = []
    for d in dims:
        if d == axis:
            index.append(at)
        elif axis == "y" and d == "yh":
            index.append(at // 2)
        elif axis == "y" and d == "yl":
            index.append(lax.rem(at, 2))
        else:
            index.append(slice(None))
    return ref.at[tuple(index)]


def dims_after(order, n):
    dims = ["x", "yh", "yl", "z"]
    for axis in order[:n]:
        for d in ("yh", "yl") if axis == "y" else (axis,):
            dims.remove(d)
    return dims


SIZES = {"x": 4, "yh": 2, "yl": 2, "z": 4}


def lead(order, n):
    return tuple(SIZES[d] for d in dims_after(order, n))


def send(src, dst, sems, index, to):
    return pltpu.make_async_remote_copy(
        src_ref=src, dst_ref=dst, send_sem=sems[0].at[index], recv_sem=sems[1].at[index],
        device_id=to, device_id_type=MESH_ID,
    )


def load_side(qkv_ref, m, keys, values, keys_t, values_t, seg_col):
    for s in range(N_CTX):
        at = slice(s * TOK, (s + 1) * TOK)
        key_t = qkv_ref[s, m, HEAD : 2 * HEAD, :]
        value_t = qkv_ref[s, m, 2 * HEAD : 3 * HEAD, :]
        keys[at, :] = key_t.T
        if values is not None:
            values[at, :] = value_t.T
        if keys_t is not None:
            keys_t[:, at] = key_t
        if values_t is not None:
            values_t[:, at] = value_t
        seg = qkv_ref[s, m, 3 * HEAD : 3 * HEAD + 1, :].astype(f32)
        seg_col[at, :] = jnp.broadcast_to(seg, (TOK, TOK)).T


def pair(ref, m, j, rows):
    return jnp.concatenate([ref[2 * j, m, rows, :], ref[2 * j + 1, m, rows, :]], axis=1)


def query_forward(held, m, j, out, full, lse_out, keys, values_t, seg_col, scores):
    query_t = pair(held, m, j, slice(0, HEAD))
    seg_row = pair(held, m, j, slice(3 * HEAD, 3 * HEAD + 1)).astype(f32)
    top = jnp.full((1, BLK), NEG_LARGE, f32)
    for k in range(NBLK):
        at = slice(k * BLK, (k + 1) * BLK)
        s = dot(keys[at, :], query_t) * SCALE2
        col = seg_col[at, :]
        same = jnp.concatenate([col, col], axis=1) == seg_row
        s = jnp.where(same, s, NEG_LARGE)
        scores[at, :] = s
        top = jnp.maximum(top, jnp.max(s, axis=0, keepdims=True))
    total = jnp.zeros((1, BLK), f32)
    acc = jnp.zeros((HEAD, BLK), f32)
    for k in range(NBLK):
        at = slice(k * BLK, (k + 1) * BLK)
        p = jnp.exp2(scores[at, :] - top)
        total = total + jnp.sum(p, axis=0, keepdims=True)
        acc = acc + dot(values_t[:, at], p.astype(bf16))
    acc = acc / total
    lse = top + jnp.log2(total)
    for half in range(2):
        cols = slice(half * TOK, (half + 1) * TOK)
        out[2 * j + half, m] = acc[:, cols].astype(bf16)
        full[2 * j + half, m] = acc[:, cols]
        lse_out[2 * j + half, m] = lse[:, cols]


GROUP_COLS = (1536, 2048, 2048, 512)
GROUP_AT = (0, 2048, 4096, 1536)
SPLITS = ((512, 1024), (1024, 1536), (1024, 1536), (128, 256))
N_COPY = 31
GROUPS = (3, 1, 2)
BEFORE = tuple((0, op) for op in ("z1", "x1", "z2", "y1", "z3", "x2", "x3", "y2", "z4", "x4", "x5"))
BEFORE += tuple((g, op) for op in ("z1", "z2", "y1") for g in GROUPS)
BEFORE += tuple((0, op) for op in ("y3", "z5", "sx", "sy", "sz", "got"))
PUSHED = tuple((g, op) for op in ("z3", "x1", "x2", "x3") for g in GROUPS)
STEPS = {
    0: tuple((g, "z4") for g in GROUPS),
    1: tuple((g, "y2") for g in GROUPS),
    3: tuple((g, "x4") for g in GROUPS),
    6: tuple((g, "x5") for g in GROUPS),
    9: tuple((g, "y3") for g in GROUPS),
    12: tuple((g, "z5") for g in GROUPS),
}
LAST = (
    tuple((g, op) for g in (3, 1) for op in ("sx", "sy", "sz")) + ((3, "got"),),
    tuple((2, op) for op in ("sx", "sy", "sz")) + ((1, "got"),),
    ((2, "got"),),
)


def ctx_device(t):
    return {"yl": t // 8, "z": lax.rem(t // 2, 4), "core": lax.rem(t, 2)}


def rows_at(start, size):
    return pl.ds(pl.multiple_of(start, 16), size)


class Gather:
    def __init__(self, g, shard, dest, sems, base, local_sem):
        core = lax.axis_index("core")
        x, z = lax.axis_index("x"), lax.axis_index("z")
        yh, yl = lax.axis_index("yh"), lax.axis_index("yl")
        y = yh * 2 + yl
        every = slice(None)
        zq, half = rows_at(z * 32, 32), rows_at(yl * 64, 64)
        cross = {"yh": 1 - yh, "yl": 1 - yl}
        count = [0]
        x_end, y_end = SPLITS[g]
        x_cols, y_cols, z_cols = slice(0, x_end), slice(x_end, y_end), slice(y_end, GROUP_COLS[g])

        def given(rows, cols):
            return shard.at[rows, GROUP_AT[g] + cols.start : GROUP_AT[g] + cols.stop]

        def make(src, dst, to):
            copy = send(src, dst, sems, base + count[0], to)
            count[0] += 1
            return copy

        def own(rows, cols, to):
            return make(given(rows, cols), dest(core, x, yh, rows, cols), to)

        def pass_on(xs, yhs, rows, cols, to):
            view = dest(core, xs, yhs, rows, cols)
            return make(view, view, to)

        x_to = {step: peer("x", step)[0] for step in (1, 2, 3)}
        y_to = {step: peer("y", step)[0] for step in (1, 3)}
        z_to = {step: peer("z", step)[0] for step in (1, 3)}
        x_before, x_after = lax.rem(x + 3, 4), lax.rem(x + 1, 4)
        y_before, y_after = lax.rem(y + 3, 4), lax.rem(y + 1, 4)
        z_before, z_after = lax.rem(z + 3, 4), lax.rem(z + 1, 4)
        self.copies = {
            "x1": [own(every, x_cols, cross)],
            "x2": [own(every, x_cols, x_to[s]) for s in (1, 3)],
            "z1": [own(zq, z_cols, cross)],
            "z2": [own(zq, z_cols, x_to[s]) for s in (1, 3, 2)],
            "y1": [own(half, y_cols, x_to[s]) for s in (1, 3, 2)],
            "x3": [pass_on(x, 1 - yh, every, x_cols, x_to[s]) for s in (1, 3)],
            "z3": [pass_on(x, 1 - yh, zq, z_cols, x_to[s]) for s in (1, 3, 2)],
            "y2": [pass_on(every, yh, half, y_cols, y_to[s]) for s in (1, 3)],
            "z4": [pass_on(every, every, zq, z_cols, z_to[s]) for s in (1, 3)],
            "x4": [
                pass_on(x_before, yh, slice(0, 64), x_cols, x_to[1]),
                pass_on(x_after, yh, slice(64, 128), x_cols, x_to[3]),
            ],
            "x5": [
                pass_on(x_before, 1 - yh, slice(0, 64), x_cols, x_to[1]),
                pass_on(x_after, 1 - yh, slice(64, 128), x_cols, x_to[3]),
            ],
            "y3": [
                pass_on(every, y_before // 2, rows_at(lax.rem(y_before, 2) * 64, 32), y_cols, y_to[1]),
                pass_on(every, y_after // 2, rows_at(lax.rem(y_after, 2) * 64 + 32, 32), y_cols, y_to[3]),
            ],
            "z5": [
                pass_on(every, every, rows_at(z_before * 32, 16), z_cols, z_to[1]),
                pass_on(every, every, rows_at(z_after * 32 + 16, 16), z_cols, z_to[3]),
            ],
        }
        for name, cols in (("sx", x_cols), ("sy", y_cols), ("sz", z_cols)):
            self.copies[name] = [pass_on(every, every, every, cols, {"core": 1 - core})]
        self.places = [
            pltpu.make_async_copy(given(rows, cols), dest(core, x, yh, rows, cols), local_sem.at[3 * g + n])
            for n, (rows, cols) in enumerate(((every, x_cols), (half, y_cols), (zq, z_cols)))
        ]

    needs = {
        "x3": ("x1",), "z3": ("z1",), "y2": ("y1",), "z4": ("z2", "z3"), "x4": ("x2",), "x5": ("x3",), "y3": ("y2",),
        "z5": ("z4",), "sx": ("x4", "x5"), "sy": ("y3",), "sz": ("z5",),
    }

    def step(self, name):
        if name == "got":
            for copy in (*self.copies["sx"], *self.copies["sy"], *self.copies["sz"]):
                copy.wait_recv()
            return
        if name == "end":
            for copies in self.copies.values():
                for copy in copies:
                    copy.wait_send()
            return
        for need in self.needs.get(name, ()):
            for copy in self.copies[need]:
                copy.wait_recv()
        if name == "z1":
            for copy in self.places:
                copy.start()
        if name == "z3":
            for copy in self.places:
                copy.wait()
        for copy in self.copies[name]:
            copy.start()


def greet_all():
    barrier = pltpu.get_barrier_semaphore()
    place = lax.axis_index(CTX)
    others = [ctx_device(lax.rem(place + d, N_CTX)) for d in range(1, N_CTX)]
    others += [peer(axis, step)[0] for axis in ("x", "y") for step in (1, 2, 3)]
    for other in others:
        pl.semaphore_signal(barrier, inc=1, device_id=other, device_id_type=MESH_ID)
    pl.semaphore_wait(barrier, len(others))


def front_kernel(
    w_attn, w_ffn, vectors, dest_ref, lengths, x_ref, cot_ref,
    out_attn, out_held, out_full, out_lse,
    out_ref, one_ref, x_t, o_t, h_t, f_t, a_low_ref, du_ref, g_ref, vec_ref, ready_ref,
    wa, w_one, w_two, w_out, vecs, small, ready, held, mixed, out_t, keys, values_t, seg_col, scores,
    mixed_rows, normal_one, slope, total, stage, shard, vec_shard, seg_ref,
    ag_send, ag_recv, vec_send, vec_recv, q_send, q_recv, o_send, o_recv, local_sem, out_sem, in_sem,
):
    core = lax.axis_index("core")
    place = lax.axis_index(CTX)
    x, yh, yl = lax.axis_index("x"), lax.axis_index("yh"), lax.axis_index("yl")

    weights = (wa, w_one, w_two, w_out)

    def dest(g):
        def view(c, xs, yhs, rows, cols):
            return weights[g].at[c, xs, yhs, rows, cols]

        return view

    gathers = [
        Gather(g, shard, dest(g), (ag_send, ag_recv), g * N_COPY, local_sem) for g in range(4)
    ]
    vec_sems = (vec_send, vec_recv)
    vec_cross = send(vec_shard, vecs.at[x, yh], vec_sems, 0, {"yh": 1 - yh, "yl": 1 - yl})
    vec_x = [send(vec_shard, vecs.at[x, yh], vec_sems, s, peer("x", s)[0]) for s in (1, 2, 3)]
    vec_x2 = [
        send(vecs.at[x, 1 - yh], vecs.at[x, 1 - yh], vec_sems, 3 + s, peer("x", s)[0]) for s in (1, 2, 3)
    ]
    fetches = []
    for g in range(4):
        start = (0, 0, FF, 3 * D)[g] + core * GROUP_COLS[g]
        source = w_ffn if g in (1, 2) else w_attn
        fetches.append(
            pltpu.make_async_copy(
                source.at[:, pl.ds(pl.multiple_of(start, 512), GROUP_COLS[g])],
                stage.at[:, GROUP_AT[g] : GROUP_AT[g] + GROUP_COLS[g]], in_sem.at[g],
            )
        )
        fetches[g].start()
    vec_shard[...] = jnp.concatenate([vectors[...], jnp.zeros((4, TOK), f32)], axis=0).astype(bf16)
    for m in range(MB):
        end = jnp.zeros((1, 1), jnp.int32)
        seg = jnp.zeros((1, TOK), jnp.int32)
        for j in range(8):
            end = end + lengths[m : m + 1, j : j + 1]
            seg = seg + jnp.where(dest_ref[m : m + 1, :] >= end, 1, 0)
        seg_ref[m] = jnp.broadcast_to(seg.astype(f32), (16, TOK)).astype(bf16)
    greet_all()
    for g in range(4):
        fetches[g].wait()
    shard[...] = stage[...].astype(bf16)
    for copy in (vec_cross, *vec_x):
        copy.start()
    done = set()

    def stages(todo):
        for g, n in todo:
            if (g, n) not in done:
                done.add((g, n))
                gathers[g].step(n)

    stages(BEFORE[:4])
    vecs[x, yh] = vec_shard[...]
    for s in range(N_CTX):
        ready[s, :, 3 * HEAD :, :] = seg_ref[...]
    vec_cross.wait_recv()
    for copy in vec_x2:
        copy.start()
    stages(BEFORE)
    vec_cross.wait_send()
    for copy in (*vec_x, *vec_x2):
        copy.wait()
    for f in range(N_FSDP):
        small[:, f * TOK : (f + 1) * TOK] = vecs[f // 2, f % 2].astype(f32)

    for part in range(6):
        c, col = part // 3, (part % 3) * 512
        kind, first = part // 2, (part % 2) * 8
        value = jnp.zeros((ROWS, 512), f32)
        weight = wa[c, :, :, :, col : col + 512].reshape(D, 512)
        value = dot(x_ref[...], weight)
        if kind != 1:
            row = 0 if kind == 0 else 1
            value = value + small[row : row + 1, first * HEAD : first * HEAD + 512]
        value = value.T.astype(bf16)
        for h in range(8):
            for m in range(MB):
                ready[first + h, m, kind * HEAD : (kind + 1) * HEAD, :] = value[
                    h * HEAD : (h + 1) * HEAD, m * TOK : (m + 1) * TOK
                ]
    swaps = [[], []]
    for m in range(MB):
        for d in range(1, N_CTX):
            t = lax.rem(place + d, N_CTX)
            swaps[m].append(send(ready.at[t, m], held.at[place, m], (q_send, q_recv), m * N_CTX + d, ctx_device(t)))
            swaps[m][-1].start()
    held[place] = ready[place]
    returns = [[], []]
    for m in range(MB):
        for d in range(1, N_CTX):
            t = lax.rem(place + d, N_CTX)
            returns[m].append(
                send(out_t.at[t, m], mixed.at[place, m], (o_send, o_recv), m * N_CTX + d, ctx_device(t))
            )
    stages(PUSHED)
    outs = [(wa.at[c], out_attn.at[:, :, :, c * 1536 : (c + 1) * 1536]) for c in range(2)]
    outs = [pltpu.make_async_copy(src, dst, out_sem.at[n]) for n, (src, dst) in enumerate(outs)]
    for copy in outs:
        copy.start()
    for m in range(MB):
        for copy in swaps[m]:
            copy.wait_recv()
        load_side(held, m, keys, None, None, values_t, seg_col)

        def query_block(j, _, m=m):
            for at, todo in STEPS.items():
                if at // NBLK == m:

                    @pl.when(j == at % NBLK)
                    def _(todo=todo):
                        stages(todo)

            query_forward(held, m, j, out_t, out_full, out_lse, keys, values_t, seg_col, scores)
            return 0

        lax.fori_loop(0, NBLK, query_block, 0)
        for copy in returns[m]:
            copy.start()
        mixed[place, m] = out_t[place, m]
    outs.append(pltpu.make_async_copy(held, out_held, out_sem.at[4]))
    outs[-1].start()

    def before(n):
        stages(LAST[n])

    for m in range(MB):
        for copy in returns[m]:
            copy.wait_recv()
    dense_part(
        mixed, x_ref, cot_ref, seg_ref, small, w_out, w_one, w_two, before,
        out_ref, one_ref, x_t, o_t, h_t, f_t, a_low_ref, du_ref, g_ref, vec_ref, ready_ref,
        mixed_rows, normal_one, slope, total,
    )
    for m in range(MB):
        for copy in (*swaps[m], *returns[m]):
            copy.wait_send()
    stages([(g, "end") for g in (0, *GROUPS)])
    for copy in outs:
        copy.wait()


def front(w_attn, w_ffn, vectors, dest, lengths, x, cot):
    vmem = pl.BlockSpec(memory_space=pltpu.VMEM)
    hbm = pl.BlockSpec(memory_space=pl.ANY)
    sem = lambda n: pltpu.SemaphoreType.DMA((n,))
    turned = jax.ShapeDtypeStruct((D, ROWS), bf16)
    return pl.pallas_call(
        front_kernel,
        in_specs=[hbm, hbm, vmem, vmem, vmem, vmem, vmem],
        out_specs=[hbm, hbm] + [vmem] * 13,
        out_shape=[
            jax.ShapeDtypeStruct((4, 2, TOK, 3 * D), bf16),
            jax.ShapeDtypeStruct((N_CTX, MB, SENT, TOK), bf16),
            jax.ShapeDtypeStruct((N_CTX, MB, HEAD, TOK), f32),
            jax.ShapeDtypeStruct((N_CTX, MB, 1, TOK), f32),
            jax.ShapeDtypeStruct((ROWS, D), bf16),
            jax.ShapeDtypeStruct((ROWS, D), f32),
            turned, turned, turned, turned,
            jax.ShapeDtypeStruct((ROWS, D), bf16),
            jax.ShapeDtypeStruct((ROWS, FF), bf16),
            jax.ShapeDtypeStruct((ROWS, FF), bf16),
            jax.ShapeDtypeStruct((N_FSDP, 16, TOK), f32),
            jax.ShapeDtypeStruct((HEADS, MB, HEAD, TOK), bf16),
        ],
        scratch_shapes=[
            *(pltpu.VMEM((2, 4, 2, TOK, GROUP_COLS[g]), bf16) for g in range(4)),
            pltpu.VMEM((4, 2, 16, TOK), bf16),
            pltpu.VMEM((16, D), f32),
            pltpu.VMEM((N_CTX, MB, SENT, TOK), bf16),
            pltpu.VMEM((N_CTX, MB, SENT, TOK), bf16),
            pltpu.VMEM((N_CTX, MB, HEAD, TOK), bf16),
            pltpu.VMEM((N_CTX, MB, HEAD, TOK), bf16),
            pltpu.VMEM((PACK, HEAD), bf16),
            pltpu.VMEM((HEAD, PACK), bf16),
            pltpu.VMEM((PACK, TOK), f32),
            pltpu.VMEM((PACK, BLK), f32),
            pltpu.VMEM((ROWS, D), bf16),
            pltpu.VMEM((ROWS, D), f32),
            pltpu.VMEM((ROWS, FF), f32),
            pltpu.VMEM((ROWS, D), f32),
            pltpu.VMEM((TOK, 6144), f32),
            pltpu.VMEM((TOK, 6144), bf16),
            pltpu.VMEM((16, TOK), bf16),
            pltpu.VMEM((MB, 16, TOK), bf16),
            sem(4 * N_COPY), sem(4 * N_COPY), sem(7), sem(7), sem(32), sem(32), sem(32), sem(32),
            sem(12), sem(6), sem(4),
        ],
        compiler_params=pltpu.CompilerParams(
            collective_id=2, has_side_effects=True, vmem_limit_bytes=60 * 2**20
        ),
        cost_estimate=pl.CostEstimate(
            flops=4 * MB * PACK * PACK * HEAD + 2 * ROWS * D * (5 * D + 4 * FF), bytes_accessed=32 * 2**20,
            transcendentals=MB * PACK * PACK,
        ),
        name="front",
    )(w_attn, w_ffn, vectors, dest, lengths, x, cot)


def back_kernel(
    left_x, left_o, left_h, left_f, right_o, right_u, right_g, vec, grad_ready, held_in, full, lse, w_qkv,
    out_attn, out_ffn, out_vec, out_sq, out_x,
    peer_left, own_right, peer_right, own_vec, peer_vec,
    *rest_refs,
):
    stores, rest_refs = rest_refs[:24], rest_refs[24:]
    (
    gathered, sq_z, sq_y, sq_x, sq_c,
    held, grad_held, out_t, landed, right_q, keys, values, keys_t, seg_col, acc_kv, square_acc, w_part,
    swap_send, swap_recv, ring_send, ring_recv, gather_send, gather_recv, sq_send, sq_recv,
    o_send, o_recv, q_send, q_recv, local_sem, out_sem,
    ) = rest_refs
    core = lax.axis_index("core")
    other = 1 - core
    place = lax.axis_index(CTX)
    row_place = lax.axis_index("yl") * 4 + lax.axis_index("z")
    lefts = (left_x, left_o, left_h, left_f)
    rights = (None, right_o, right_u, right_g)
    to_core = {"core": other}

    fetch = pltpu.make_async_copy(held_in, held, local_sem.at[0])
    fetch.start()
    fetches = [fetch]
    for i in range(1, 4):
        cols = pl.ds(pl.multiple_of(core * WIDTHS[i], 512), WIDTHS[i])
        fetches.append(
            pltpu.make_async_copy(
                rights[i].at[:, cols], own_right.at[:, OFFSETS[i] : OFFSETS[i] + WIDTHS[i]], local_sem.at[i]
            )
        )
        fetches[-1].start()
    greet_all()

    pushes, returns = [[], []], [[], []]
    for m in range(MB):
        for d in range(1, N_CTX):
            t = lax.rem(place + d, N_CTX)
            to = ctx_device(t)
            pushes[m].append(
                send(grad_ready.at[t, m], grad_held.at[place, m], (o_send, o_recv), m * N_CTX + d, to)
            )
            returns[m].append(send(out_t.at[t, m], landed.at[place, m], (q_send, q_recv), m * N_CTX + d, to))
    swaps = []
    for i in (2, 3, 1, 0):
        swaps.append(send(lefts[i], peer_left.at[i], (swap_send, swap_recv), 2 * i, to_core))
        if i:
            from_cols = pl.ds(pl.multiple_of(other * WIDTHS[i], 512), WIDTHS[i])
            swaps.append(
                send(
                    rights[i].at[:, from_cols], peer_right.at[:, OFFSETS[i] : OFFSETS[i] + WIDTHS[i]],
                    (swap_send, swap_recv), 2 * i + 1, to_core,
                )
            )
    for m in range(MB):
        for copy in pushes[m]:
            copy.start()
    for copy in swaps:
        copy.start()
    grad_held[place] = grad_ready[place]
    for copy in fetches:
        copy.wait()

    late = [(p, N_EARLY[p] * COLS, COLS) for p in range(3)] + [(0, VEC_AT, 128)]
    early = [(p, b * COLS, COLS) for p, b in EARLY]

    def number(p, at, width):
        return 12 if width != COLS else PART_AT[p] // COLS + at // COLS

    def store(kind, p, at, width):
        return stores[4 * kind + 3].at[0] if width != COLS else stores[4 * kind + p].at[at // COLS]

    def copies(p, phase, at, width):
        order = ORDERS[p]
        axis = order[phase]
        out = []
        for step in (1, 2, 3):
            to, index = peer(axis, step)
            chunk = pick(store(phase, p, at, width), axis, index, dims_after(order, phase))
            land = store(3 + phase, p, at, width).at[step - 1]
            out.append(
                send(
                    chunk, land, (ring_send, ring_recv), 39 + 39 * phase + number(p, at, width) * 3 + step - 1, to
                )
            )
        return out

    def first_copies(p, at, width):
        order = ORDERS[p]
        axis = order[0]
        n = lead(order, 1)[0]
        halves = (slice(0, n // 2), slice(n // 2, n))
        (up, up_at), (_, far_at), (down, down_at) = (peer(axis, step) for step in (1, 2, 3))
        out = []
        for k, (index, half, slot, to) in enumerate(
            (
                (far_at, 0, 2, up), (far_at, 1, 2, down), (up_at, 1, 0, up), (down_at, 0, 1, down),
                (up_at, 0, 0, up), (down_at, 1, 1, down),
            )
        ):
            chunk = pick(store(0, p, at, width), axis, index, dims_after(order, 0)).at[halves[half]]
            land = store(3, p, at, width).at[slot, halves[half]]
            out.append(send(chunk, land, (ring_send, ring_recv), number(p, at, width) * 6 + k, to))
        return out

    def begin(p, at, width):
        for copy in first_copies(p, at, width)[:4]:
            copy.start()

    def relay(p, at, width):
        order = ORDERS[p]
        axis = order[0]
        n = lead(order, 1)[0]
        all_copies = first_copies(p, at, width)
        land = store(3, p, at, width)
        for half, step in ((0, 1), (1, 3)):
            all_copies[half].wait_recv()
            own = pick(store(0, p, at, width), axis, peer(axis, step)[1], dims_after(order, 0))

            def add(i, _, own=own):
                own[i] = (own[i].astype(f32) + land[2, i].astype(f32)).astype(bf16)
                return 0

            lax.fori_loop(half * (n // 2), (half + 1) * (n // 2), add, 0)
            all_copies[4 + half].start()

    def multiply(p, b):
        i, col = PRODUCT[(p, b)]
        if i == 0:
            mine = right_q.at[:, pl.ds(pl.multiple_of(core * WIDTHS[0] + col, 512), COLS)]
        else:
            mine = own_right.at[:, OFFSETS[i] + col : OFFSETS[i] + col + COLS]
        theirs = peer_right.at[:, OFFSETS[i] + col : OFFSETS[i] + col + COLS]

        def rows_block(x, _):
            rows = pl.ds(pl.multiple_of(x * 256, 256), 256)
            value = dot(lefts[i][rows, :], mine[...]) + dot(peer_left[i, rows, :], theirs[...])
            stores[p][b, x] = value.astype(bf16).reshape(2, 2, 4, 16, COLS)
            return 0

        lax.fori_loop(0, 4, rows_block, 0)

    def reduce(phase, p, at, width):
        order = ORDERS[p]
        axis = order[phase]
        land = store(3 + phase, p, at, width)
        if phase == 0:
            all_copies = first_copies(p, at, width)
            for copy in all_copies[:2]:
                copy.wait_send()
            for copy in all_copies[2:]:
                copy.wait()
        else:
            for copy in copies(p, phase, at, width):
                copy.wait()
        own = pick(store(phase, p, at, width), axis, coordinate(axis), dims_after(order, phase))
        if phase < 2:
            dst = store(phase + 1, p, at, width)

            def add(n, _):
                value = own[n].astype(f32)
                for step in range(3 if phase else 2):
                    value = value + land[step, n].astype(f32)
                dst[n] = value.astype(bf16)
                return 0

            lax.fori_loop(0, lead(order, phase + 1)[0], add, 0)
            for copy in copies(p, phase + 1, at, width):
                copy.start()
            return
        value = own[...].astype(f32)
        for step in range(3):
            value = value + land[step].astype(f32)
        to = PART_AT[p] + at if width == COLS else 6144
        gathered[core, row_place, :, to : to + width] = value.astype(bf16)
        square = value * value
        if width != COLS:
            square = square * jnp.where(core == 0, 1.0, 0.0)
        squares = square_acc[...]
        for c in range(0, width, 128):
            squares = squares + square[:8, c : c + 128] + square[8:, c : c + 128]
        square_acc[...] = squares

    def run_task(phase, p, b):
        if phase == "relay":
            relay(p, b * COLS, COLS)
        else:
            reduce(phase, p, b * COLS, COLS)

    square_acc[...] = jnp.zeros_like(square_acc)
    for copy in swaps:
        copy.wait()
    for p, at, width in early:
        multiply(p, at // COLS)
        begin(p, at, width)

    for m in range(MB):
        load_side(held, m, keys, values, keys_t, None, seg_col)
        acc_kv[...] = jnp.zeros_like(acc_kv)
        for copy in pushes[m]:
            copy.wait_recv()

        def query_block(j, _, m=m):
            for at, tasks in TASKS.items():
                if at // NBLK == m:

                    @pl.when(j == at % NBLK)
                    def _(tasks=tasks):
                        for phase, p, b in tasks:
                            run_task(phase, p, b)

            query_t = pair(held, m, j, slice(0, HEAD))
            seg_row = pair(held, m, j, slice(3 * HEAD, 3 * HEAD + 1)).astype(f32)
            grad_t = pair(grad_held, m, j, slice(0, HEAD))
            row_lse = pair(lse, m, j, slice(0, 1))
            delta = jnp.sum(grad_t.astype(f32) * pair(full, m, j, slice(0, HEAD)), axis=0, keepdims=True)
            acc_q = jnp.zeros((HEAD, BLK), f32)
            none = jnp.zeros((BLK, HEAD), bf16)
            sides = jnp.concatenate(
                [jnp.concatenate([query_t.T, none], axis=1), jnp.concatenate([none, grad_t.T], axis=1)], axis=0
            )
            block = lambda k: slice(k * BLK, (k + 1) * BLK)
            ahead = (dot(keys[block(0), :], query_t), dot(values[block(0), :], grad_t))
            behind = None
            for k in range(NBLK + 1):
                if k < NBLK:
                    at = block(k)
                    s, dp = ahead
                    if k + 1 < NBLK:
                        ahead = (dot(keys[block(k + 1), :], query_t), dot(values[block(k + 1), :], grad_t))
                if behind is not None:
                    to, ds, pb = behind
                    acc_q = acc_q + dot(keys_t[:, to], ds)
                    acc_kv[to, :] += dot(jnp.concatenate([ds, pb], axis=1), sides)
                if k < NBLK:
                    col = seg_col[at, :]
                    same = jnp.concatenate([col, col], axis=1) == seg_row
                    p = jnp.exp2(jnp.where(same, s * SCALE2 - row_lse, NEG_LARGE))
                    behind = (at, (p * (dp - delta)).astype(bf16), p.astype(bf16))
            acc_q = (acc_q * SCALE).astype(bf16)
            out_t[2 * j, m, :HEAD, :] = acc_q[:, :TOK]
            out_t[2 * j + 1, m, :HEAD, :] = acc_q[:, TOK:]
            return 0

        lax.fori_loop(0, NBLK, query_block, 0)
        for s in range(N_CTX):
            at = slice(s * TOK, (s + 1) * TOK)
            both = acc_kv[at, :].T
            out_t[s, m, HEAD : 2 * HEAD, :] = (both[:HEAD] * SCALE).astype(bf16)
            out_t[s, m, 2 * HEAD :, :] = both[HEAD:].astype(bf16)
        for copy in returns[m]:
            copy.start()
        landed[place, m] = out_t[place, m]

    fetch_w = [
        pltpu.make_async_copy(w_qkv.at[:, n * COLS : (n + 1) * COLS], w_part.at[n % 2], local_sem.at[4 + n])
        for n in range(6)
    ]
    done = [task for tasks in TASKS.values() for task in tasks]
    for phase in ("relay", 0, 1):
        for p, b in EARLY:
            if (phase, p, b) not in done:
                run_task(phase, p, b)
    gives = []
    for m in range(MB):
        for copy in pushes[m]:
            copy.wait_send()
        for copy in returns[m]:
            copy.wait()
        if m == 0:
            fetch_w[0].start()
            fetch_w[1].start()
        for i in range(HEADS // 2):
            for kind in range(3):
                rows = slice(kind * HEAD, (kind + 1) * HEAD)
                both = jnp.concatenate([landed[2 * i, m, rows, :], landed[2 * i + 1, m, rows, :]], axis=0)
                right_q[m * TOK : (m + 1) * TOK, kind * D + i * 128 : kind * D + (i + 1) * 128] = both.T
        rows = slice(m * TOK, (m + 1) * TOK)
        gives.append(
            send(
                right_q.at[rows, pl.ds(pl.multiple_of(other * WIDTHS[0], 512), WIDTHS[0])],
                peer_right.at[rows, 0 : WIDTHS[0]], (swap_send, swap_recv), (1, 9)[m], to_core,
            )
        )
        gives[m].start()
    sum_q = jnp.sum(right_q[:, :D].astype(f32), axis=0, keepdims=True)
    sum_v = jnp.sum(right_q[:, 2 * D :].astype(f32), axis=0, keepdims=True)
    row = lax.broadcasted_iota(jnp.int32, (16, TOK), 0)
    own_vec[...] = jnp.zeros_like(own_vec)
    for f in range(N_FSDP):
        cols = slice(f * TOK, (f + 1) * TOK)
        value = jnp.where(row == 0, sum_q[:, cols], jnp.where(row == 1, sum_v[:, cols], vec[f]))
        own_vec[f // 2, f % 2, 0, 0] = value.astype(bf16)
    give_vec = send(own_vec, peer_vec, (swap_send, swap_recv), 8, to_core)
    give_vec.start()
    for copy in gives:
        copy.wait()
    for p, at, width in late:
        if width == COLS:
            multiply(p, at // COLS)
        else:
            give_vec.wait()
            stores[3][0] = (own_vec[...].astype(f32) + peer_vec[...].astype(f32)).astype(bf16)
        begin(p, at, width)
    for n in range(6):
        fetch_w[n].wait()
        part = dot_nt(right_q[:, n * COLS : (n + 1) * COLS], w_part[n % 2])
        if n == 0:
            out_x[...] = part
        else:
            out_x[...] += part
        if n < 4:
            fetch_w[n + 2].start()
    for piece in late:
        relay(*piece)
    for piece in early:
        reduce(2, *piece)
    for phase in range(3):
        for piece in late:
            reduce(phase, *piece)
    squares = square_acc[...]
    yl, z = lax.axis_index("yl"), lax.axis_index("z")
    z_first, y_first = slice(0, HALF_Z), slice(HALF_Z, 6272)
    to_y = {"yl": 1 - yl}
    gather_sems = (gather_send, gather_recv)
    sq_sems = (sq_send, sq_recv)

    def spread(buffer, axis, base):
        at = coordinate(axis)
        out = []
        for step in (1, 2, 3):
            out.append(send(buffer.at[at], buffer.at[at], sq_sems, base + step - 1, peer(axis, step)[0]))
        return out

    def total(buffer):
        return (buffer[0] + buffer[1]) + (buffer[2] + buffer[3])

    sq_z[z] = squares
    squares_z = spread(sq_z, "z", 0)
    first_z = [
        send(gathered.at[core, row_place, :, z_first], gathered.at[core, row_place, :, z_first], gather_sems, step - 1, peer("z", step)[0])
        for step in (1, 2, 3)
    ]
    first_y = send(gathered.at[core, row_place, :, y_first], gathered.at[core, row_place, :, y_first], gather_sems, 3, to_y)
    for copy in (*squares_z, *first_z, first_y):
        copy.start()
    for copy in squares_z:
        copy.wait()
    y_at = coordinate("y")
    sq_y[y_at] = total(sq_z)
    squares_y = spread(sq_y, "y", 3)
    for copy in squares_y:
        copy.start()
    for copy in (*first_z, first_y):
        copy.wait()
    quarter = pl.ds(yl * 4, 4)
    second_y = send(
        gathered.at[core, quarter, :, z_first], gathered.at[core, quarter, :, z_first], gather_sems, 4, to_y
    )
    second_y.start()
    second_z = []
    for step in (1, 2, 3):
        for half in range(2):
            view = gathered.at[core, half * 4 + z, :, y_first]
            second_z.append(send(view, view, gather_sems, 5 + (step - 1) * 2 + half, peer("z", step)[0]))
    for copy in second_z:
        copy.start()
    for copy in squares_y:
        copy.wait()
    x_at = coordinate("x")
    sq_x[x_at] = total(sq_y)
    squares_x = spread(sq_x, "x", 6)
    for copy in squares_x:
        copy.start()
    for copy in squares_x:
        copy.wait()
    sq_c[core] = total(sq_x)
    square_c = send(sq_c.at[core], sq_c.at[core], sq_sems, 9, to_core)
    square_c.start()
    square_c.wait()
    out_sq[...] = sq_c[0] + sq_c[1]
    second_y.wait()
    for copy in second_z:
        copy.wait()
    last = send(gathered.at[core], gathered.at[core], gather_sems, 11, to_core)
    last.start()
    last.wait()
    locals_ = []
    for c in range(2):
        for p in range(3):
            for b in range(N_EARLY[p] + 1):
                i, col = PRODUCT[(p, b)]
                target, base = ((out_attn, 0), (out_attn, 3072), (out_ffn, 0), (out_ffn, FF))[i]
                base = base + c * WIDTHS[i] + col
                at = PART_AT[p] + b * COLS
                locals_.append(
                    pltpu.make_async_copy(
                        gathered.at[c, :, :, at : at + COLS], target.at[:, :, base : base + COLS],
                        out_sem.at[len(locals_)],
                    )
                )
    locals_.append(pltpu.make_async_copy(gathered.at[0, :, :, 6144:], out_vec, out_sem.at[len(locals_)]))
    for copy in locals_:
        copy.start()
    for copy in locals_:
        copy.wait()


def back(lefts, rights, vec, grad_ready, held, full, lse, w_qkv):
    vmem = pl.BlockSpec(memory_space=pltpu.VMEM)
    hbm = pl.BlockSpec(memory_space=pl.ANY)
    scratch = [
        pltpu.VMEM((4, D, ROWS), bf16),
        pltpu.VMEM((ROWS, 6144), bf16),
        pltpu.VMEM((ROWS, 6144), bf16),
        pltpu.VMEM((4, 2, 2, 4, 16, 128), bf16),
        pltpu.VMEM((4, 2, 2, 4, 16, 128), bf16),
    ]
    for kind in range(6):
        n = kind if kind < 3 else kind - 2
        for p, count, width in (*((p, N_EARLY[p] + 1, COLS) for p in range(3)), (0, 1, 128)):
            landing = (3,) if kind >= 3 else ()
            scratch.append(pltpu.VMEM((count, *landing, *lead(ORDERS[p], n), 16, width), bf16))
    scratch += [
        pltpu.VMEM((2, 8, 16, 6272), bf16),
        pltpu.VMEM((4, 8, 128), f32),
        pltpu.VMEM((4, 8, 128), f32),
        pltpu.VMEM((4, 8, 128), f32),
        pltpu.VMEM((2, 8, 128), f32),
        pltpu.VMEM((N_CTX, MB, SENT, TOK), bf16),
        pltpu.VMEM((N_CTX, MB, HEAD, TOK), bf16),
        pltpu.VMEM((N_CTX, MB, 3 * HEAD, TOK), bf16),
        pltpu.VMEM((N_CTX, MB, 3 * HEAD, TOK), bf16),
        pltpu.VMEM((ROWS, 3 * D), bf16),
        pltpu.VMEM((PACK, HEAD), bf16),
        pltpu.VMEM((PACK, HEAD), bf16),
        pltpu.VMEM((HEAD, PACK), bf16),
        pltpu.VMEM((PACK, TOK), f32),
        pltpu.VMEM((PACK, 2 * HEAD), f32),
        pltpu.VMEM((8, 128), f32),
        pltpu.VMEM((2, D, COLS), bf16),
    ]
    for count in (10, 10, 156, 156, 12, 12, 10, 10, 32, 32, 32, 32, 10, 25):
        scratch.append(pltpu.SemaphoreType.DMA((count,)))
    out = pl.pallas_call(
        back_kernel,
        in_specs=[vmem] * 4 + [hbm] * 3 + [vmem, vmem, hbm, vmem, vmem, hbm],
        out_specs=[hbm, hbm, hbm, vmem, vmem],
        out_shape=[
            jax.ShapeDtypeStruct((8, 16, 4 * D), bf16),
            jax.ShapeDtypeStruct((8, 16, 2 * FF), bf16),
            jax.ShapeDtypeStruct((8, 16, 128), bf16),
            jax.ShapeDtypeStruct((8, 128), f32),
            jax.ShapeDtypeStruct((ROWS, D), f32),
        ],
        scratch_shapes=scratch,
        compiler_params=pltpu.CompilerParams(
            collective_id=1, has_side_effects=True, vmem_limit_bytes=60 * 2**20
        ),
        cost_estimate=pl.CostEstimate(
            flops=2 * 512 * D * 6144 + 10 * MB * PACK * PACK * HEAD, bytes_accessed=16 * 2**20,
            transcendentals=MB * PACK * PACK,
        ),
        name="back",
    )(*lefts, *rights, vec, grad_ready, held, full, lse, w_qkv)
    return out[0].reshape(TOK, 4 * D), out[1].reshape(TOK, 2 * FF), out[2], out[3], out[4]


def layer_stats(values, gain_row, shift_row):
    center = values - jnp.mean(values, axis=-1, keepdims=True)
    inverse = lax.rsqrt(jnp.mean(center * center, axis=-1, keepdims=True) + NORM_EPS)
    normal = center * inverse
    return (normal * gain_row + shift_row, normal, inverse)


def layer_back(grad_value, normal, inverse, gain_row):
    scaled = grad_value * gain_row
    return inverse * (
        scaled
        - jnp.mean(scaled, axis=-1, keepdims=True)
        - normal * jnp.mean(scaled * normal, axis=-1, keepdims=True)
    )


N_CHUNK = 8
CHUNK = FF // N_CHUNK
ERF_TOP = (
    -2.72614225801306e-10, 2.77068142495902e-08, -2.10102402082508e-06, -5.69250639462346e-05,
    -7.34990630326855e-04, -2.95459980854025e-03, -1.60960333262415e-02,
)
ERF_LOW = (
    -1.45660718464996e-05, -2.13374055278905e-04, -1.68282697438203e-03, -7.37332916720468e-03,
    -1.42647390514189e-02,
)


def erf(value):
    value = jnp.clip(value, -4.0, 4.0)
    square = value * value
    top, low = jnp.full_like(square, ERF_TOP[0]), jnp.full_like(square, ERF_LOW[0])
    for c in ERF_TOP[1:]:
        top = top * square + c
    for c in ERF_LOW[1:]:
        low = low * square + c
    return value * top / low


def w_block(ref, n):
    per = ref.shape[-1] // CHUNK
    at = (n % per) * CHUNK
    return ref[n // per, :, :, :, at : at + CHUNK].reshape(D, CHUNK)


def dense_part(
    mixed_ref, x_ref, cot_ref, seg_ref, small_ref, w_out, w_one, w_two, before,
    out_ref, one_ref, x_t, o_t, h_t, f_t, a_low_ref, du_ref, g_ref, vec_ref, ready_ref,
    mixed, normal_one_ref, slope, total,
):
    def row(i):
        return small_ref[i : i + 1, :]

    def put(i, value):
        for f in range(N_FSDP):
            vec_ref[f, i : i + 1, :] = value[:, f * TOK : (f + 1) * TOK]

    def sums(value):
        return jnp.sum(value, axis=0, keepdims=True)

    vec_ref[...] = jnp.zeros_like(vec_ref)
    for m in range(MB):
        tok = slice(m * TOK, (m + 1) * TOK)
        for i in range(HEADS // 2):
            both = jnp.concatenate([mixed_ref[2 * i, m], mixed_ref[2 * i + 1, m]], axis=0)
            o_t[i * 128 : (i + 1) * 128, tok] = both
            mixed[tok, i * 128 : (i + 1) * 128] = both.T
    before(0)
    branch = jnp.concatenate([dot(mixed[...], w_block(w_out, n)) for n in range(2)], axis=1)
    normed_one, normal_one, inverse_one = layer_stats(x_ref[...].astype(f32) + branch + row(2), row(4), row(5))
    normal_one_ref[...] = normal_one
    normed_low = normed_one.astype(bf16)
    h_t[...] = normed_low.T
    total[...] = normed_one + row(3)
    before(1)
    for n in range(N_CHUNK):
        cols = slice(n * CHUNK, (n + 1) * CHUNK)
        bias = small_ref[8 + n // 2 : 9 + n // 2, (n % 2) * CHUNK : (n % 2 + 1) * CHUNK]
        u = dot(normed_low, w_block(w_one, n)) + bias
        share = 0.5 + 0.5 * erf(u * math.sqrt(0.5))
        g_ref[:, cols] = (u * share).astype(bf16)
        slope[:, cols] = share + u * (jnp.exp(-0.5 * u * u) * (1.0 / math.sqrt(2.0 * math.pi)))
    before(2)
    for n in range(N_CHUNK):
        total[...] += dot_nt(g_ref[:, n * CHUNK : (n + 1) * CHUNK], w_block(w_two, n))
    output, normal_two, inverse_two = layer_stats(total[...], row(6), row(7))
    keep = []
    for m in range(MB):
        inside = jnp.where(seg_ref[m, 0:1, :].astype(f32) < 8.0, 1.0, 0.0)
        keep.append(jnp.broadcast_to(inside, (TOK, TOK)).T[:, 0:1])
    keep = jnp.concatenate(keep, axis=0)
    out_ref[...] = (output * keep).astype(bf16)
    grad_out = cot_ref[...].astype(f32) * keep
    put(6, sums(grad_out * normal_two))
    put(7, sums(grad_out))
    grad_two = layer_back(grad_out, normal_two, inverse_two, row(6))
    f_low = grad_two.astype(bf16)
    f_t[...] = f_low.T
    put(3, sums(f_low.astype(f32)))
    total[...] = grad_two
    for n in range(N_CHUNK):
        cols = slice(n * CHUNK, (n + 1) * CHUNK)
        du = (dot(f_low, w_block(w_two, n)) * slope[:, cols]).astype(bf16)
        du_ref[:, cols] = du
        part = sums(du.astype(f32))
        for i in range(CHUNK // TOK):
            f = (n % 2) * (CHUNK // TOK) + i
            vec_ref[f, 8 + n // 2 : 9 + n // 2, :] = part[:, i * TOK : (i + 1) * TOK]
        total[...] += dot_nt(du, w_block(w_one, n))
    grad_normed = total[...]
    normal_one = normal_one_ref[...]
    put(4, sums(grad_normed * normal_one))
    put(5, sums(grad_normed))
    grad_one = layer_back(grad_normed, normal_one, inverse_one, row(4))
    one_ref[...] = grad_one
    a_low = grad_one.astype(bf16)
    a_low_ref[...] = a_low
    put(2, sums(a_low.astype(f32)))
    for n in range(2):
        part = a_low[:, n * CHUNK : (n + 1) * CHUNK]
        part = dot_nt(part, w_block(w_out, n))
        grad_mixed = part if n == 0 else grad_mixed + part
    grad_mixed = grad_mixed.T.astype(bf16)
    for h in range(HEADS):
        for m in range(MB):
            ready_ref[h, m] = grad_mixed[h * HEAD : (h + 1) * HEAD, m * TOK : (m + 1) * TOK]
    x_t[...] = x_ref[...].T


def adamw(weight, grad_value, first, second, rate, decay):
    first_new = BETA_FIRST * first + (1.0 - BETA_FIRST) * grad_value
    second_new = BETA_SECOND * second + (1.0 - BETA_SECOND) * grad_value * grad_value
    first_hat = first_new * (1.0 / (1.0 - BETA_FIRST**STEP))
    second_hat = second_new * (1.0 / (1.0 - BETA_SECOND**STEP))
    weight_new = weight - rate * (first_hat / (jnp.sqrt(second_hat) + ADAM_EPS) + decay * weight)
    return (weight_new, first_new, second_new)


def finish_kernel(
    squares, grad_vec, grad_attn, grad_ffn, aw, am, av, fw, fm, fv, vw, vm, vv, one, grad_x, y,
    norm, aw_new, am_new, av_new, fw_new, fm_new, fv_new, vw_new, vm_new, vv_new, a_copy, f_copy, bias, dx, y_out,
):
    total = jnp.sum(jnp.sum(squares[...], axis=0, keepdims=True), axis=1, keepdims=True)
    root = jnp.sqrt(total)
    norm[...] = root
    factor = jnp.minimum(1.0, CLIP_NORM / (root + 1e-06))
    rate = D ** (-0.5)
    for grad, ins, outs, low, scale in (
        (grad_attn, (aw, am, av), (aw_new, am_new, av_new), a_copy, ATTN_RATE_SCALE * rate),
        (grad_ffn, (fw, fm, fv), (fw_new, fm_new, fv_new), f_copy, rate),
    ):
        for at in range(0, grad.shape[1], 1024):
            cols = slice(at, at + 1024)
            weight, first, second = adamw(
                ins[0][:, cols], grad[:, cols].astype(f32) * factor, ins[1][:, cols], ins[2][:, cols], scale,
                WEIGHT_DECAY,
            )
            outs[0][:, cols] = weight
            outs[1][:, cols] = first
            outs[2][:, cols] = second
            low[:, cols] = weight.astype(bf16)
    clipped = grad_vec[0].astype(f32) * factor
    vw_new[...], vm_new[...], vv_new[...] = adamw(
        vw[...], clipped[:12], vm[...], vv[...], RATE_VECTOR, 0.0
    )
    bias[...] = clipped[2:3]
    dx[...] = (one[...] + grad_x[...]).astype(bf16)
    y_out[...] = y[...]


def finish(squares, grad_vec, grad_attn, grad_ffn, attn, ffn, vec, one, grad_x, y):
    steps = 8
    rows = TOK // steps
    whole = lambda a: pl.BlockSpec(a.shape, lambda i: (0,) * len(a.shape))
    part = lambda a: pl.BlockSpec((a.shape[0] // steps, a.shape[1]), lambda i: (i, 0))
    shape = lambda a, dt=f32: jax.ShapeDtypeStruct(a.shape, dt)
    ins = [squares, grad_vec, grad_attn, grad_ffn, *attn, *ffn, *vec, one, grad_x, y]
    specs = [whole(squares), pl.BlockSpec((1, 16, TOK), lambda i: (0, 0, 0)), part(grad_attn), part(grad_ffn)]
    specs += [part(a) for a in (*attn, *ffn)] + [whole(a) for a in vec] + [part(a) for a in (one, grad_x, y)]
    outs = [jax.ShapeDtypeStruct((1, 1), f32), *(shape(a) for a in (*attn, *ffn, *vec))]
    outs += [shape(attn[0], bf16), shape(ffn[0], bf16), jax.ShapeDtypeStruct((1, TOK), f32), shape(one, bf16), shape(y, bf16)]
    out_specs = [whole(outs[0]), *(part(a) for a in outs[1:7]), *(whole(a) for a in outs[7:10])]
    out_specs += [part(outs[10]), part(outs[11]), whole(outs[12]), part(outs[13]), part(outs[14])]
    return pl.pallas_call(
        finish_kernel,
        grid=(steps,),
        in_specs=specs,
        out_specs=out_specs,
        out_shape=outs,
        compiler_params=pltpu.CompilerParams(vmem_limit_bytes=60 * 2**20),
        cost_estimate=pl.CostEstimate(flops=40 * 12 * D * TOK, bytes_accessed=44 * 2**20, transcendentals=24 * D * TOK),
        name="finish",
    )(*ins)


def shards(
    tokens, cotangent, dest, lengths, attn_weight, attn_first, attn_second,
    ffn_weight, ffn_first, ffn_second, vectors, vec_first, vec_second,
):
    x = tokens.reshape(ROWS, D)
    cot = cotangent.reshape(ROWS, D)
    (
        w_qkv, held, mixed_full, lse, output, grad_one, x_t, o_t, h_t, f_t, a_low, du, g, vec_rows, grad_ready,
    ) = front(attn_weight, ffn_weight, vectors, dest[:, 0], lengths[:, 0], x, cot)
    grad_attn, grad_ffn, grad_vec, squares, grad_x = back(
        (x_t, o_t, h_t, f_t),
        (a_low, du, g),
        vec_rows,
        grad_ready,
        held,
        mixed_full,
        lse,
        w_qkv.reshape(D, 3 * D),
    )
    (
        norm, aw, am, av, fw, fm, fv, vw, vm, vv, a_copy, f_copy, bias, input_grad, output,
    ) = finish(
        squares, grad_vec, grad_attn, grad_ffn,
        (attn_weight, attn_first, attn_second), (ffn_weight, ffn_first, ffn_second),
        (vectors, vec_first, vec_second), grad_one, grad_x, output,
    )
    return (
        output.reshape(tokens.shape), input_grad.reshape(tokens.shape), norm.reshape(()),
        aw, am, av, fw, fm, fv, vw, vm, vv, a_copy, f_copy, bias.reshape(TOK),
    )


def solution(mesh):
    fine = Mesh(mesh.devices.reshape(2, 4, 2, 4, 2), ("yl", "z", "core", "x", "yh"))
    act = P(None, FSDP, CTX, None)
    row = P(FSDP, None)
    col = P(None, FSDP)
    return jax.shard_map(
        shards,
        mesh=fine,
        in_specs=(act, act, P(None, FSDP, CTX), P(None, FSDP, None), row, row, row, row, row, row, col, col, col),
        out_specs=(act, act, P(), row, row, row, row, row, row, col, col, col, row, row, P(FSDP)),
        check_vma=False,
    )
```

profile of v0, /device:TPU:1, one launch (start us, length us, event | category | flops | bytes accessed | tf_op | source)
XLA Modules:
  0.0 259.5 jit_solution(4810830491152642047)
XLA Ops:
  0.6 116.4 %front.1 = (bf16[4,2,128,3072]{3,2,1,0:T(8,128)(2,1)}, bf16[16,2,208,128]{3,2,1,0:T(8,128)(2,1)}, f32[16,2,64,128]{3,2,1,0:T(8,128)}, f32[16,2,1,128]{3,2,1,0:T(...) custom-call(f32[128,4096]{1,0:T(8,128)} %aw.1, ...), custom_call_target="tpu_custom_call" | custom-call | flops 13421772800 | bytes 33554432 | tf_op jit(solution)/shard_map/front/pallas_call | solution.py:470
  117.0 123.6 %back.1 = (bf16[8,16,4096]{2,1,0:T(8,128)(2,1)}, bf16[8,16,8192]{2,1,0:T(8,128)(2,1)}, bf16[8,16,128]{2,1,0:T(8,128)(2,1)}, f32[8,128]{1,0:T(8,128)}, f32[256,1024]{1,0:T(8,128)}) custom-call(bf16[1024,256]{1,0:T(8,128)(2,1)} %get-tuple-element.50.left_x, bf16[1024,256]{1,0:T(8,128)(2,1)} %get-tuple-element.51.left_o, ...), custom_call_target="tpu_custom_call" | custom-call | flops 11811160064 | bytes 16777216 | tf_op jit(solution)/shard_map/back/pallas_call | solution.py:966
  240.7 18.4 %finish.1 = (f32[1,1]{1,0:T(1,128)}, f32[128,4096]{1,0:T(8,128)}, f32[128,4096]{1,0:T(8,128)}, f32[128,4096]{1,0:T(8,128)}, f32[128,8192]{1,0:T(8,128)}, /*index...) custom-call(f32[8,128]{1,0:T(8,128)} %get-tuple-element.63.squares, ...), custom_call_target="tpu_custom_call" | custom-call | flops 62914560 | bytes 46137344 | tf_op jit(solution)/shard_map/finish/pallas_call | solution.py:1173
where the time goes:
time: 264 us; the launch traced here: 260 us
  Pallas kernels  258 us (98%)
    pallas_call x1, Pallas kernels, back(): pl.pallas_call(back_kernel, in_specs=[vmem] * 4 + [hbm] * 3 + [vmem, vmem...  124 us
    pallas_call x1, Pallas kernels, front(): pl.pallas_call(front_kernel, in_specs=[hbm, hbm, vmem, vmem, vmem, vmem,...  116 us
    pallas_call x1, Pallas kernels, finish(): pl.pallas_call(finish_kernel, grid=(steps,), in_specs=specs, out_specs=ou...  18.4 us

commit v1 on v0

--- a/solution.py
+++ b/solution.py
@@ -1062,10 +1062,13 @@
     h_t[...] = normed_low.T
     total[...] = normed_one + row(3)
     before(1)
+    ahead = dot(normed_low, w_block(w_one, 0))
     for n in range(N_CHUNK):
         cols = slice(n * CHUNK, (n + 1) * CHUNK)
         bias = small_ref[8 + n // 2 : 9 + n // 2, (n % 2) * CHUNK : (n % 2 + 1) * CHUNK]
-        u = dot(normed_low, w_block(w_one, n)) + bias
+        u = ahead + bias
+        if n + 1 < N_CHUNK:
+            ahead = dot(normed_low, w_block(w_one, n + 1))
         share = 0.5 + 0.5 * erf(u * math.sqrt(0.5))
         g_ref[:, cols] = (u * share).astype(bf16)
         slope[:, cols] = share + u * (jnp.exp(-0.5 * u * u) * (1.0 / math.sqrt(2.0 * math.pi)))
@@ -1087,16 +1090,21 @@
     f_t[...] = f_low.T
     put(3, sums(f_low.astype(f32)))
     total[...] = grad_two
+    ahead = dot(f_low, w_block(w_two, 0))
     for n in range(N_CHUNK):
         cols = slice(n * CHUNK, (n + 1) * CHUNK)
-        du = (dot(f_low, w_block(w_two, n)) * slope[:, cols]).astype(bf16)
+        product = ahead
+        if n + 1 < N_CHUNK:
+            ahead = dot(f_low, w_block(w_two, n + 1))
+        if n:
+            total[...] += dot_nt(du, w_block(w_one, n - 1))
+        du = (product * slope[:, cols]).astype(bf16)
         du_ref[:, cols] = du
         part = sums(du.astype(f32))
         for i in range(CHUNK // TOK):
             f = (n % 2) * (CHUNK // TOK) + i
             vec_ref[f, 8 + n // 2 : 9 + n // 2, :] = part[:, i * TOK : (i + 1) * TOK]
-        total[...] += dot_nt(du, w_block(w_one, n))
-    grad_normed = total[...]
+    grad_normed = total[...] + dot_nt(du, w_block(w_one, N_CHUNK - 1))
     normal_one = normal_one_ref[...]
     put(4, sums(grad_normed * normal_one))
     put(5, sums(grad_normed))

time: 264 us -> 264 us (level)
  no operation moved by 1% of the time
where the time goes in v1:
time: 264 us; the launch traced here: 259 us
  Pallas kernels  258 us (98%)
    pallas_call x1, Pallas kernels, back(): pl.pallas_call(back_kernel, in_specs=[vmem] * 4 + [hbm] * 3 + [vmem, vmem...  124 us
    pallas_call x1, Pallas kernels, front(): pl.pallas_call(front_kernel, in_specs=[hbm, hbm, vmem, vmem, vmem, vmem,...  116 us
    pallas_call x1, Pallas kernels, finish(): pl.pallas_call(finish_kernel, grid=(steps,), in_specs=specs, out_specs=ou...  18.4 us

profile of v1, /device:TPU:1, one launch (start us, length us, event | category | flops | bytes accessed | tf_op | source)
XLA Modules:
  0.0 259.1 jit_solution(17904172686502359735)
XLA Ops:
  0.6 115.8 %front.1 = (bf16[4,2,128,3072]{3,2,1,0:T(8,128)(2,1)}, bf16[16,2,208,128]{3,2,1,0:T(8,128)(2,1)}, f32[16,2,64,128]{3,2,1,0:T(8,128)}, f32[16,2,1,128]{3,2,1,0:T(...) custom-call(f32[128,4096]{1,0:T(8,128)} %aw.1, ...), custom_call_target="tpu_custom_call" | custom-call | flops 13421772800 | bytes 33554432 | tf_op jit(solution)/shard_map/front/pallas_call | solution.py:470
  116.5 123.8 %back.1 = (bf16[8,16,4096]{2,1,0:T(8,128)(2,1)}, bf16[8,16,8192]{2,1,0:T(8,128)(2,1)}, bf16[8,16,128]{2,1,0:T(8,128)(2,1)}, f32[8,128]{1,0:T(8,128)}, f32[256,1024]{1,0:T(8,128)}) custom-call(bf16[1024,256]{1,0:T(8,128)(2,1)} %get-tuple-element.50.left_x, bf16[1024,256]{1,0:T(8,128)(2,1)} %get-tuple-element.51.left_o, ...), custom_call_target="tpu_custom_call" | custom-call | flops 11811160064 | bytes 16777216 | tf_op jit(solution)/shard_map/back/pallas_call | solution.py:966
  240.3 18.4 %finish.1 = (f32[1,1]{1,0:T(1,128)}, f32[128,4096]{1,0:T(8,128)}, f32[128,4096]{1,0:T(8,128)}, f32[128,4096]{1,0:T(8,128)}, f32[128,8192]{1,0:T(8,128)}, /*index...) custom-call(f32[8,128]{1,0:T(8,128)} %get-tuple-element.63.squares, ...), custom_call_target="tpu_custom_call" | custom-call | flops 62914560 | bytes 46137344 | tf_op jit(solution)/shard_map/finish/pallas_call | solution.py:1181
